TPU v7x, 128 devices: a whole 4x4x4 slice. The times are simulated.
128 devices in a mesh: level: 4 (over x), grp: 32 (over z, y, core).
Axes of the slice: x: 4, y: 4, z: 4, core: 2. Of those that a mesh axis runs over, the one named last changes fastest.
Arguments:
- x_old: bfloat16 [4, 512, 16, 128], P('level', 'grp'), may hold values from -6 to 6
- rhs: float32 [4, 512, 16, 128], P('level', 'grp'), may hold values from -6 to 6
- down_tiles: bfloat16 [4, 512, 6, 128, 128], P('level', 'grp'), may hold values from -0.4375 to 0.4375
- level_tiles: bfloat16 [4, 512, 6, 128, 128], P('level', 'grp'), may hold values from -0.1875 to 0.1875
- up_tiles: bfloat16 [4, 512, 6, 128, 128], P('level', 'grp'), may hold values from -0.1875 to 0.1875
- inverses: float32 [4, 512, 128, 128], P('level', 'grp'), as said below
- tile_cols: int32 [4, 512, 3, 6], P('level', 'grp'), may hold values from 0 to 511
- tile_counts: int32 [4, 512, 3], P('level', 'grp'), may hold values from 1 to 6, as said below
Outputs:
- solution: float32 [4, 512, 16, 128], P('level', 'grp')
Inputs may be any that keep to these rules, and one draw needn't show every extreme that they name: `tile_counts`: slots at or beyond a block row's count are to be ignored; every level has a block row with 6 live slots in every band. `inverses`: each inverse is an arbitrary dense matrix given in full.
All inputs are finite; a program needn't handle non-finite values.
Results may differ from a plain program's by a relative error of at most 0.0015.
Values may be sent and summed in bfloat16 or wider, within the bound.
A program may use at most 64 MiB of HBM per device.

v0:
```python
import jax
import jax.numpy as jnp
from jax import lax
from jax.sharding import PartitionSpec as P


def from_behind(value, axis, by):
    length = lax.axis_size(axis)
    pairs = [(i, i + by) for i in range(length) if 0 <= i + by < length]
    return lax.ppermute(value, axis, pairs)


def band_term(tiles, cols, counts, source):
    pieces = source[cols]
    slots = jnp.arange(cols.shape[1], dtype=jnp.int32)
    live = slots[None, :] < counts[:, None]
    pieces = jnp.where(live[:, :, None, None], pieces, jnp.zeros((), pieces.dtype))
    return jnp.einsum("bkrc,bkcq->brq", pieces, tiles, preferred_element_type=jnp.float32)


def solve_blocks(resid, inverse):
    return jnp.einsum(
        "brc,bcq->brq",
        resid,
        inverse,
        precision=lax.Precision.HIGHEST,
        preferred_element_type=jnp.float32,
    )


def shards(x_old, rhs, down_tiles, level_tiles, up_tiles, inverses, tile_cols, tile_counts):
    own = x_old[0]
    whole = lax.all_gather(own, "grp", axis=0, tiled=True)
    above = from_behind(whole, "level", -1)
    cols = tile_cols[0]
    counts = tile_counts[0]
    base = rhs[0] - band_term(level_tiles[0], cols[:, 1], counts[:, 1], whole)
    base = base - band_term(up_tiles[0], cols[:, 2], counts[:, 2], above)
    inverse = inverses[0]
    down_here = down_tiles[0]
    first = solve_blocks(base, inverse)

    def level_turn(turn, current):
        outgoing = current.astype(jnp.bfloat16)
        gathered = lax.all_gather(outgoing, "grp", axis=0, tiled=True)
        panel = from_behind(gathered, "level", 1)
        resid = base - band_term(down_here, cols[:, 0], counts[:, 0], panel)
        return solve_blocks(resid, inverse)

    final = lax.fori_loop(1, lax.axis_size("level"), level_turn, first)
    return final[None]


def solution(mesh):
    return jax.shard_map(
        shards,
        mesh=mesh,
        in_specs=(
            P("level", "grp", None, None),
            P("level", "grp", None, None),
            P("level", "grp", None, None, None),
            P("level", "grp", None, None, None),
            P("level", "grp", None, None, None),
            P("level", "grp", None, None),
            P("level", "grp", None, None),
            P("level", "grp", None),
        ),
        out_specs=P("level", "grp", None, None),
        check_vma=False,
    )
```

profile of v0, /device:TPU:2, one launch (start us, length us, event | category | flops | bytes accessed | tf_op | source)
XLA Modules:
  0.0 425.3 jit_solution(5996172280538096552)
XLA Ops:
  7.3 48.8 %all-gather.4.cloned.1.call-done = bf16[1,512,16,128]{3,2,0,1:T(8,128)(2,1)} async-done(((bf16[1,16,16,128]{3,2,0,1:T(8,128)(2,1)}), bf16[1,512,16,128]{3,2,0,1:T(8,128)(2,1)}) %all-gather.4.cloned.1.call-update) | async-done | bytes 2097168 | tf_op jit(solution)/shard_map/all_gather | solution.py:33
  56.0 2.5 collective-permute-start.1
  58.5 1.3 copy.28
  62.1 2.3 gather_fusion.1
  64.3 2.1 fusion.18
  66.5 39.5 %collective-permute-done.1 = bf16[512,16,128]{2,1,0:T(8,128)(2,1)} collective-permute-done((bf16[512,16,128]{2,1,0:T(8,128)(2,1)}, bf16[512,16,128]{2,1,0:T(8,128)(2,1)}, u32[]{:S(2)}, u32[]{:S(2)}) %collective-permute-start.1) | collective-permute-done | bytes 2097184 | tf_op jit(solution)/shard_map/ppermute | solution.py:10
  106.0 2.3 gather_fusion.2
  108.3 2.5 fusion.15
  111.8 306.3 %while.10 = (s32[]{:T(128)}, f32[16,16,128]{2,1,0:T(8,128)S(1)}, s32[16,3]{0,1:T(4,128)}, s32[16,3,6]{0,1,2:T(4,128)}, bf16[16,6,128,128]{3,2,1,0:T(8,128)(2,1)}...) while((s32[]{:T(128)}, f32[16,16,128]{2,1,0:T(8,128)S(1)}, s32[16,3]{0,1:T(4,128)}, ...), condition=%wide.region_1.2_spmd, body=%wide.region_0.1_spmd.sunk | while | flops 100926848 | bytes 25173568 | solution.py:50
  112.6 45.6 %all-gather.6.cloned.1.call-done = bf16[512,16,128]{2,1,0:T(8,128)(2,1)} async-done(((bf16[16,16,128]{2,1,0:T(8,128)(2,1)}), bf16[512,16,128]{2,1,0:T(8,128)(2,1)}) %all-gather.6.cloned.1.call-update) | async-done | bytes 2097168 | tf_op jit(solution)/shard_map/while/body/eval_jaxpr/all_gather | solution.py:45
  158.2 3.4 collective-permute-start
  163.2 45.0 %collective-permute-done = bf16[512,16,128]{2,1,0:T(8,128)(2,1)} collective-permute-done((bf16[512,16,128]{2,1,0:T(8,128)(2,1)}, bf16[512,16,128]{2,1,0:T(8,128)(2,1)}, u32[]{:S(2)}, u32[]{:S(2)}) %collective-permute-start) | collective-permute-done | bytes 2097184 | tf_op jit(solution)/shard_map/while/body/eval_jaxpr/ppermute | solution.py:10
  208.2 2.3 gather_fusion
  210.5 2.5 fusion.46
  214.8 45.6 %all-gather.6.cloned.1.call-done = bf16[512,16,128]{2,1,0:T(8,128)(2,1)} async-done(((bf16[16,16,128]{2,1,0:T(8,128)(2,1)}), bf16[512,16,128]{2,1,0:T(8,128)(2,1)}) %all-gather.6.cloned.1.call-update) | async-done | bytes 2097168 | tf_op jit(solution)/shard_map/while/body/eval_jaxpr/all_gather | solution.py:45
  260.4 3.4 collective-permute-start
  265.4 45.0 %collective-permute-done = bf16[512,16,128]{2,1,0:T(8,128)(2,1)} collective-permute-done((bf16[512,16,128]{2,1,0:T(8,128)(2,1)}, bf16[512,16,128]{2,1,0:T(8,128)(2,1)}, u32[]{:S(2)}, u32[]{:S(2)}) %collective-permute-start) | collective-permute-done | bytes 2097184 | tf_op jit(solution)/shard_map/while/body/eval_jaxpr/ppermute | solution.py:10
  310.4 2.3 gather_fusion
  312.7 2.5 fusion.46
  316.9 45.4 %all-gather.6.cloned.1.call-done = bf16[512,16,128]{2,1,0:T(8,128)(2,1)} async-done(((bf16[16,16,128]{2,1,0:T(8,128)(2,1)}), bf16[512,16,128]{2,1,0:T(8,128)(2,1)}) %all-gather.6.cloned.1.call-update) | async-done | bytes 2097168 | tf_op jit(solution)/shard_map/while/body/eval_jaxpr/all_gather | solution.py:45
  362.3 3.4 collective-permute-start
  367.3 45.0 %collective-permute-done = bf16[512,16,128]{2,1,0:T(8,128)(2,1)} collective-permute-done((bf16[512,16,128]{2,1,0:T(8,128)(2,1)}, bf16[512,16,128]{2,1,0:T(8,128)(2,1)}, u32[]{:S(2)}, u32[]{:S(2)}) %collective-permute-start) | collective-permute-done | bytes 2097184 | tf_op jit(solution)/shard_map/while/body/eval_jaxpr/ppermute | solution.py:10
  412.3 2.3 gather_fusion
  414.6 2.5 fusion.46
  (59 shorter events, 14.6 us)
Async XLA Ops:
  6.5 57.8 %copy-start = (bf16[1,16,6,128,128]{4,3,2,1,0:T(8,128)(2,1)S(1)}, bf16[1,16,6,128,128]{4,3,2,1,0:T(8,128)(2,1)}, u32[]{:S(2)}) copy-start(bf16[1,16,6,128,128]{4,3,2,1,0:T(8,128)(2,1)} %param.13) | copy-start | bytes 9437188
  6.5 49.5 %all-gather.4.cloned.1.call-start = ((), (), s32[]{:S(2)}) async-start(), calls=%async_computation | async-start | bytes 2162688 | tf_op jit(solution)/shard_map/all_gather | solution.py:33
  56.0 50.0 %collective-permute-start.1 = (bf16[512,16,128]{2,1,0:T(8,128)(2,1)}, bf16[512,16,128]{2,1,0:T(8,128)(2,1)}, u32[]{:S(2)}, u32[]{:S(2)}) collective-permute-start(bf16[512,16,128]{2,1,0:T(8,128)(2,1)} %bitcast.92), channel_id=1, source_target_pairs={{32,0},{64,32},{96,64},{33,1},{65,33},{97,65},{34,2},{66,34},{98,6... | collective-permute-start | bytes 6291464 | tf_op jit(solution)/shard_map/ppermute | solution.py:10
  61.4 0.6 copy-start.5
  108.3 2.6 copy-start.1
  110.8 1.0 copy-start.3
  111.8 46.4 %all-gather.6.cloned.1.call-start = ((), (), s32[]{:S(2)}) async-start(), calls=%async_computation.1 | async-start | bytes 2162688 | tf_op jit(solution)/shard_map/while/body/eval_jaxpr/all_gather | solution.py:45
  158.2 50.0 %collective-permute-start = (bf16[512,16,128]{2,1,0:T(8,128)(2,1)}, bf16[512,16,128]{2,1,0:T(8,128)(2,1)}, u32[]{:S(2)}, u32[]{:S(2)}) collective-permute-start(bf16[512,16,128]{2,1,0:T(8,128)(2,1)} %all-gather.6.cloned.1.call-done), channel_id=1, source_target_pairs={{0,32},{32,64},{64,96},{1,33},{33,65},{65,97},{2,34},{34,66},{66,9... | collective-permute-start | bytes 6291464 | tf_op jit(solution)/shard_map/while/body/eval_jaxpr/ppermute | solution.py:10
  210.5 2.6 copy-start.2
  214.0 46.4 %all-gather.6.cloned.1.call-start = ((), (), s32[]{:S(2)}) async-start(), calls=%async_computation.1 | async-start | bytes 2162688 | tf_op jit(solution)/shard_map/while/body/eval_jaxpr/all_gather | solution.py:45
  260.4 50.0 %collective-permute-start = (bf16[512,16,128]{2,1,0:T(8,128)(2,1)}, bf16[512,16,128]{2,1,0:T(8,128)(2,1)}, u32[]{:S(2)}, u32[]{:S(2)}) collective-permute-start(bf16[512,16,128]{2,1,0:T(8,128)(2,1)} %all-gather.6.cloned.1.call-done), channel_id=1, source_target_pairs={{0,32},{32,64},{64,96},{1,33},{33,65},{65,97},{2,34},{34,66},{66,9... | collective-permute-start | bytes 6291464 | tf_op jit(solution)/shard_map/while/body/eval_jaxpr/ppermute | solution.py:10
  312.7 2.6 copy-start.2
  316.2 46.1 %all-gather.6.cloned.1.call-start = ((), (), s32[]{:S(2)}) async-start(), calls=%async_computation.1 | async-start | bytes 2162688 | tf_op jit(solution)/shard_map/while/body/eval_jaxpr/all_gather | solution.py:45
  362.3 50.0 %collective-permute-start = (bf16[512,16,128]{2,1,0:T(8,128)(2,1)}, bf16[512,16,128]{2,1,0:T(8,128)(2,1)}, u32[]{:S(2)}, u32[]{:S(2)}) collective-permute-start(bf16[512,16,128]{2,1,0:T(8,128)(2,1)} %all-gather.6.cloned.1.call-done), channel_id=1, source_target_pairs={{0,32},{32,64},{64,96},{1,33},{33,65},{65,97},{2,34},{34,66},{66,9... | collective-permute-start | bytes 6291464 | tf_op jit(solution)/shard_map/while/body/eval_jaxpr/ppermute | solution.py:10
  414.5 2.6 copy-start.2
  418.1 0.7 copy-start.4
Sparse Core Ops, SparseCore 0:
  9.6 46.3 all-gather.3
  114.9 43.2 all-gather.5
  217.1 43.2 all-gather.5
  319.0 43.2 all-gather.5
where the time goes:
time: 426 us; the launch traced here: 425 us
  waiting for transfers between devices  361 us (85%)
  local copies, waits for them, and re-layouts  17.2 us (4%)
  matrix products  16.3 us (4%)
  between operations  13.2 us (3%)
  starting transfers between devices  12.6 us (3%)
  other arithmetic  5.17 us (1%)
    ppermute x4, waiting for transfers between devices, from_behind(): return lax.ppermute(value, axis, pairs)  174 us
    all_gather x3, waiting for transfers between devices, level_turn(): gathered = lax.all_gather(outgoing, 'grp', axis=0, tiled=True)  137 us
    all_gather x1, waiting for transfers between devices, shards(): whole = lax.all_gather(own, 'grp', axis=0, tiled=True)  48.8 us
    ppermute x4, starting transfers between devices, from_behind(): return lax.ppermute(value, axis, pairs)  12.6 us
    dot_general x5, matrix products, band_term(): jnp.einsum('bkrc,bkcq->brq', pieces, tiles, preferred_element_type=jnp.fl...  12.3 us
    gather x5, local copies, waits for them, and re-layouts, band_term(): pieces = source[cols]  11.3 us
  transfers between devices with their start and end apart: 8, of which 8 were waited for; matrix products, arithmetic and copies ran while one was open for 3% of the time, Pallas kernels for 0%

commit v1 on v0

--- a/solution.py
+++ b/solution.py
@@ -2,6 +2,11 @@
 import jax.numpy as jnp
 from jax import lax
 from jax.sharding import PartitionSpec as P
+
+
+def gather_over(block, name, dim):
+    sent = jnp.stack([block] * lax.axis_size(name))
+    return jnp.concatenate(lax.all_to_all(sent, name, 0, 0), axis=dim)
 
 
 def from_behind(value, axis, by):
@@ -42,7 +47,7 @@
 
     def level_turn(turn, current):
         outgoing = current.astype(jnp.bfloat16)
-        gathered = lax.all_gather(outgoing, "grp", axis=0, tiled=True)
+        gathered = gather_over(outgoing, "grp", 0)
         panel = from_behind(gathered, "level", 1)
         resid = base - band_term(down_here, cols[:, 0], counts[:, 0], panel)
         return solve_blocks(resid, inverse)

time: 426 us -> 387 us (0.908)
  waiting for transfers between devices: 361 us -> 223 us
  blocking collectives: 0 us -> 98.2 us
    all_gather x3 -> x0, waiting for transfers between devices: 137 us -> none  [level_turn(): gathered = lax.all_gather(outgoing, 'grp', axis=0, tiled=True)]
    all_to_all x0 -> x3, blocking collectives: none -> 98.2 us  [gather_over(): return jnp.concatenate(lax.all_to_all(sent, name, 0, 0), axis=dim)]
  transfers between devices with their start and end apart: 8 -> 5, of which waited for: 8 -> 5; matrix products, arithmetic and copies ran while one was open for 3% -> 3% of each run, Pallas kernels for 0% -> 0%
where the time goes in v1:
time: 387 us; the launch traced here: 386 us
  waiting for transfers between devices  223 us (58%)
  blocking collectives  98.2 us (25%)
  local copies, waits for them, and re-layouts  18.6 us (5%)
  matrix products  16.3 us (4%)
  between operations  13.5 us (3%)
  starting transfers between devices  12.6 us (3%)
    ppermute x4, waiting for transfers between devices, from_behind(): return lax.ppermute(value, axis, pairs)  174 us
    all_to_all x3, blocking collectives, gather_over(): return jnp.concatenate(lax.all_to_all(sent, name, 0, 0), axis=dim)  98.2 us
    all_gather x1, waiting for transfers between devices, shards(): whole = lax.all_gather(own, 'grp', axis=0, tiled=True)  48.8 us
    ppermute x4, starting transfers between devices, from_behind(): return lax.ppermute(value, axis, pairs)  12.6 us
    dot_general x5, matrix products, band_term(): jnp.einsum('bkrc,bkcq->brq', pieces, tiles, preferred_element_type=jnp.fl...  12.3 us
    gather x5, local copies, waits for them, and re-layouts, band_term(): pieces = source[cols]  11.3 us
  transfers between devices with their start and end apart: 5, of which 5 were waited for; matrix products, arithmetic and copies ran while one was open for 3% of the time, Pallas kernels for 0%

profile of v1, /device:TPU:2, one launch (start us, length us, event | category | flops | bytes accessed | tf_op | source)
XLA Modules:
  0.0 386.1 jit_solution(2795664720138875481)
XLA Ops:
  7.3 48.8 %all-gather.3.cloned.1.call-done = bf16[1,512,16,128]{3,2,0,1:T(8,128)(2,1)} async-done(((bf16[1,16,16,128]{3,2,0,1:T(8,128)(2,1)}), bf16[1,512,16,128]{3,2,0,1:T(8,128)(2,1)}) %all-gather.3.cloned.1.call-update) | async-done | bytes 2097168 | tf_op jit(solution)/shard_map/all_gather | solution.py:38
  56.0 2.5 collective-permute-start.1
  58.5 1.3 copy.28
  62.1 2.3 gather_fusion.1
  64.4 2.1 fusion.18
  66.5 39.5 %collective-permute-done.1 = bf16[512,16,128]{2,1,0:T(8,128)(2,1)} collective-permute-done((bf16[512,16,128]{2,1,0:T(8,128)(2,1)}, bf16[512,16,128]{2,1,0:T(8,128)(2,1)}, u32[]{:S(2)}, u32[]{:S(2)}) %collective-permute-start.1) | collective-permute-done | bytes 2097184 | tf_op jit(solution)/shard_map/ppermute | solution.py:15
  106.0 2.3 gather_fusion.2
  108.3 2.5 fusion.15
  111.8 266.7 %while.10 = (s32[]{:T(128)}, f32[16,16,128]{2,1,0:T(8,128)S(1)}, s32[16,3]{0,1:T(4,128)}, s32[16,3,6]{0,1,2:T(4,128)}, bf16[16,6,128,128]{3,2,1,0:T(8,128)(2,1)}...) while((s32[]{:T(128)}, f32[16,16,128]{2,1,0:T(8,128)S(1)}, s32[16,3]{0,1:T(4,128)}, ...), condition=%wide.region_1.2_spmd, body=%wide.region_0.1_spmd.sunk | while | flops 100926848 | bytes 25042456 | solution.py:55
  112.3 33.7 %all_to_all.6 = bf16[32,16,16,128]{3,2,1,0:T(8,128)(2,1)} all-to-all(bf16[32,16,16,128]{3,2,1,0:T(8,128)(2,1)S(1)} %stack.3), channel_id=1, replica_groups=mesh['level'=4,'grp'=32] {'grp'}, dimensions={0} | all-to-all | bytes 4194304 | tf_op jit(solution)/shard_map/while/body/eval_jaxpr/all_to_all | solution.py:9
  146.0 3.4 collective-permute-start
  151.1 44.8 %collective-permute-done = bf16[512,16,128]{2,1,0:T(8,128)(2,1)} collective-permute-done((bf16[512,16,128]{2,1,0:T(8,128)(2,1)}, bf16[512,16,128]{2,1,0:T(8,128)(2,1)}, u32[]{:S(2)}, u32[]{:S(2)}) %collective-permute-start) | collective-permute-done | bytes 2097184 | tf_op jit(solution)/shard_map/while/body/eval_jaxpr/ppermute | solution.py:15
  195.9 2.3 gather_fusion
  198.2 2.5 fusion.46
  202.2 32.3 %all_to_all.6 = bf16[32,16,16,128]{3,2,1,0:T(8,128)(2,1)} all-to-all(bf16[32,16,16,128]{3,2,1,0:T(8,128)(2,1)S(1)} %stack.3), channel_id=1, replica_groups=mesh['level'=4,'grp'=32] {'grp'}, dimensions={0} | all-to-all | bytes 4194304 | tf_op jit(solution)/shard_map/while/body/eval_jaxpr/all_to_all | solution.py:9
  234.5 3.4 collective-permute-start
  239.5 44.8 %collective-permute-done = bf16[512,16,128]{2,1,0:T(8,128)(2,1)} collective-permute-done((bf16[512,16,128]{2,1,0:T(8,128)(2,1)}, bf16[512,16,128]{2,1,0:T(8,128)(2,1)}, u32[]{:S(2)}, u32[]{:S(2)}) %collective-permute-start) | collective-permute-done | bytes 2097184 | tf_op jit(solution)/shard_map/while/body/eval_jaxpr/ppermute | solution.py:15
  284.3 2.3 gather_fusion
  286.6 2.5 fusion.46
  290.6 32.3 %all_to_all.6 = bf16[32,16,16,128]{3,2,1,0:T(8,128)(2,1)} all-to-all(bf16[32,16,16,128]{3,2,1,0:T(8,128)(2,1)S(1)} %stack.3), channel_id=1, replica_groups=mesh['level'=4,'grp'=32] {'grp'}, dimensions={0} | all-to-all | bytes 4194304 | tf_op jit(solution)/shard_map/while/body/eval_jaxpr/all_to_all | solution.py:9
  322.9 3.4 collective-permute-start
  327.9 44.8 %collective-permute-done = bf16[512,16,128]{2,1,0:T(8,128)(2,1)} collective-permute-done((bf16[512,16,128]{2,1,0:T(8,128)(2,1)}, bf16[512,16,128]{2,1,0:T(8,128)(2,1)}, u32[]{:S(2)}, u32[]{:S(2)}) %collective-permute-start) | collective-permute-done | bytes 2097184 | tf_op jit(solution)/shard_map/while/body/eval_jaxpr/ppermute | solution.py:15
  372.7 2.3 gather_fusion
  375.0 2.5 fusion.46
  (56 shorter events, 14.0 us)
Async XLA Ops:
  6.5 57.8 %copy-start = (bf16[1,16,6,128,128]{4,3,2,1,0:T(8,128)(2,1)S(1)}, bf16[1,16,6,128,128]{4,3,2,1,0:T(8,128)(2,1)}, u32[]{:S(2)}) copy-start(bf16[1,16,6,128,128]{4,3,2,1,0:T(8,128)(2,1)} %param.13) | copy-start | bytes 9437188
  6.5 49.5 %all-gather.3.cloned.1.call-start = ((), (), s32[]{:S(2)}) async-start(), calls=%async_computation.1 | async-start | bytes 2162688 | tf_op jit(solution)/shard_map/all_gather | solution.py:38
  56.0 50.0 %collective-permute-start.1 = (bf16[512,16,128]{2,1,0:T(8,128)(2,1)}, bf16[512,16,128]{2,1,0:T(8,128)(2,1)}, u32[]{:S(2)}, u32[]{:S(2)}) collective-permute-start(bf16[512,16,128]{2,1,0:T(8,128)(2,1)} %bitcast.95), channel_id=1, source_target_pairs={{32,0},{64,32},{96,64},{33,1},{65,33},{97,65},{34,2},{66,34},{98,6... | collective-permute-start | bytes 6291464 | tf_op jit(solution)/shard_map/ppermute | solution.py:15
  61.4 0.6 copy-start.5
  108.3 2.6 copy-start.1
  110.8 1.0 copy-start.3
  146.0 49.8 %collective-permute-start = (bf16[512,16,128]{2,1,0:T(8,128)(2,1)}, bf16[512,16,128]{2,1,0:T(8,128)(2,1)}, u32[]{:S(2)}, u32[]{:S(2)}) collective-permute-start(bf16[512,16,128]{2,1,0:T(8,128)(2,1)} %bitcast.88), channel_id=1, source_target_pairs={{0,32},{32,64},{64,96},{1,33},{33,65},{65,97},{2,34},{34,66},{66,9... | collective-permute-start | bytes 6291464 | tf_op jit(solution)/shard_map/while/body/eval_jaxpr/ppermute | solution.py:15
  198.2 2.6 copy-start.2
  234.5 49.8 %collective-permute-start = (bf16[512,16,128]{2,1,0:T(8,128)(2,1)}, bf16[512,16,128]{2,1,0:T(8,128)(2,1)}, u32[]{:S(2)}, u32[]{:S(2)}) collective-permute-start(bf16[512,16,128]{2,1,0:T(8,128)(2,1)} %bitcast.88), channel_id=1, source_target_pairs={{0,32},{32,64},{64,96},{1,33},{33,65},{65,97},{2,34},{34,66},{66,9... | collective-permute-start | bytes 6291464 | tf_op jit(solution)/shard_map/while/body/eval_jaxpr/ppermute | solution.py:15
  286.6 2.6 copy-start.2
  322.9 49.8 %collective-permute-start = (bf16[512,16,128]{2,1,0:T(8,128)(2,1)}, bf16[512,16,128]{2,1,0:T(8,128)(2,1)}, u32[]{:S(2)}, u32[]{:S(2)}) collective-permute-start(bf16[512,16,128]{2,1,0:T(8,128)(2,1)} %bitcast.88), channel_id=1, source_target_pairs={{0,32},{32,64},{64,96},{1,33},{33,65},{65,97},{2,34},{34,66},{66,9... | collective-permute-start | bytes 6291464 | tf_op jit(solution)/shard_map/while/body/eval_jaxpr/ppermute | solution.py:15
  375.0 2.6 copy-start.2
  378.6 0.7 copy-start.4
Sparse Core Ops, SparseCore 0:
  9.6 46.3 all-gather.2
